TPU v7x, 32 devices: a whole 2x2x4 slice. The times are simulated.
32 devices in a mesh: group: 2 (over y), dp: 4 (over z), tensor: 4 (over x, core).
Axes of the slice: x: 2, y: 2, z: 4, core: 2. Of those that a mesh axis runs over, the one named last changes fastest.
Arguments:
- attended: bfloat16 [1024, 8192], P(('group', 'dp'), 'tensor'), parts along dimension 0, may hold values from -6 to 6
- hidden: bfloat16 [1024, 8192], P(('group', 'dp'), 'tensor'), parts along dimension 0, may hold values from -6 to 6
- output_weight: bfloat16 [8192, 8192], P('tensor'), may hold values from -0.09375 to 0.09375
- low_rank_shrink: bfloat16 [64, 64, 8192], P(('group', 'dp'), None, 'tensor'), parts along dimension 0, may hold values from -0.0625 to 0.0625
- low_rank_expand: bfloat16 [64, 64, 8192], P(('group', 'dp'), None, 'tensor'), parts along dimension 0, may hold values from -0.75 to 0.75
- row_adapter_index: int32 [1024, 1], P(('group', 'dp')), parts along dimension 0, may hold values from 0 to 31; in each aligned block of 128 rows (0 to 127, 128 to 255, ...) at most 8 rows name the same one
- adapter_store_slot: int32 [64], P('group'), parts along dimension 0, may hold values from 0 to 31, each once
Outputs:
- mixed: bfloat16 [1024, 8192], P(('group', 'dp'), 'tensor'), parts along dimension 0
There are 2 independent parts, one for each index of `group`. A program takes and returns all parts, laid end to end along the dimension named above; an argument that names none is the same for every part. Nothing has to cross between parts.
Inputs may be any that keep to these rules, and one draw needn't show every extreme that they name: `row_adapter_index`: in the rows of one dp index (aligned blocks of 128 rows) each adapter is named at most 8 times, a bound that some block reaches. A permutation: adapter a lies in store slot adapter_store_slot[a], held by dp index adapter_store_slot[a] // 8.
All inputs are finite; a program needn't handle non-finite values.
Results may differ from a plain program's by a relative error of at most 0.0036.
Values may be sent and summed in bfloat16 or wider, within the bound.
A program may use at most 128 MiB of HBM per device.

v0:
```python
import jax
import jax.numpy as jnp
from jax import lax
from jax.sharding import PartitionSpec as P

ADAPTER_ROW_CAP = 8


def apply_low_rank(holding_buffer, shrink_store, expand_store):
    partial_rank = jnp.einsum(
        "fex,fyx->fey", holding_buffer, shrink_store, preferred_element_type=jnp.float32
    )
    shrunk_rows = lax.psum(partial_rank, "tensor").astype(jnp.bfloat16)
    expanded_rows = jnp.einsum(
        "zxb,zbl->zxl", shrunk_rows, expand_store, preferred_element_type=jnp.float32
    )
    return expanded_rows.astype(jnp.bfloat16)


def per_device(
    attended,
    hidden,
    output_weight,
    low_rank_shrink,
    low_rank_expand,
    row_adapter_index,
    adapter_store_slot,
):
    row_count = attended.shape[0]
    shard_width = attended.shape[1]
    adapter_number = adapter_store_slot.shape[0]
    base_projection_sum = lax.psum_scatter(
        lax.dot_general(
            output_weight, attended, (((0,), (1,)), ((), ())), preferred_element_type=jnp.float32
        ),
        "tensor",
        scatter_dimension=0,
        tiled=True,
    ).T
    row_adapter = row_adapter_index[:, 0]
    matches = row_adapter[:, None] == jnp.arange(adapter_number, dtype=jnp.int32)[None, :]
    row_slot = jnp.sum(jnp.where(matches, adapter_store_slot[None, :], 0), axis=1)
    earlier = jnp.tri(row_count, k=-1, dtype=bool)
    same_adapter = row_adapter[:, None] == row_adapter[None, :]
    row_place = jnp.sum(same_adapter & earlier, axis=1)
    target_rows = row_slot * ADAPTER_ROW_CAP + row_place
    holding_buffer = (
        jnp.zeros((adapter_number * ADAPTER_ROW_CAP, shard_width), jnp.bfloat16)
        .at[target_rows]
        .set(attended)
    )
    holding_buffer = holding_buffer.reshape(adapter_number, ADAPTER_ROW_CAP, shard_width)
    shrink_store, expand_store = (
        lax.all_gather(low_rank_shrink, "dp", axis=0, tiled=True),
        lax.all_gather(low_rank_expand, "dp", axis=0, tiled=True),
    )
    returned_rows = apply_low_rank(holding_buffer, shrink_store, expand_store)
    low_rank_delta = returned_rows.reshape(adapter_number * ADAPTER_ROW_CAP, shard_width)[
        target_rows
    ]
    return (
        hidden.astype(jnp.float32) + base_projection_sum + low_rank_delta.astype(jnp.float32)
    ).astype(jnp.bfloat16)


def solution(mesh):
    placed = (
        P(("group", "dp"), "tensor"),
        P(("group", "dp"), "tensor"),
        P("tensor", None),
        P(("group", "dp"), None, "tensor"),
        P(("group", "dp"), None, "tensor"),
        P(("group", "dp"), None),
        P("group"),
    )
    return jax.shard_map(
        per_device,
        mesh=mesh,
        in_specs=placed,
        out_specs=P(("group", "dp"), "tensor"),
        check_vma=False,
    )
```

profile of v0, /device:TPU:0, one launch (start us, length us, event | category | flops | bytes accessed | tf_op | source)
XLA Modules:
  0.0 327.4 jit_solution(115886992121125371)
XLA Ops:
  7.4 0.0 all-gather.3.cloned.1.call-start
  7.4 0.7 all-gather.3.cloned.1.call-update
  8.1 0.0 all-gather.5.cloned.1.call-start
  8.1 0.7 all-gather.5.cloned.1.call-update
  8.8 0.0 copy-start
  8.8 0.0 copy-start.1
  8.9 0.0 copy-start.2
  8.9 0.0 reduce-scatter.2.cloned.1.call-start
  8.9 17.0 %fusion.10 = f32[8192,128]{1,0:T(8,128)} fusion(bf16[2048,8192]{1,0:T(8,128)(2,1)} %param.9, bf16[128,2048]{1,0:T(8,128)(2,1)} %param.7), kind=kOutput, calls=%fused_computation.21 | convolution fusion | flops 4294967296 | bytes 38273024 | tf_op jit(solution)/shard_map/dot_general | solution.py:33
  25.9 0.0 reduce-scatter.2.cloned.1.call-update
  25.9 0.3 copy.17
  26.2 0.1 select_reduce_fusion
  26.3 0.2 convert_reduce_fusion
  26.5 2.2 scatter_custom_fusion
  28.7 133.5 %all-gather.3.cloned.1.call-done = bf16[32,64,2048]{2,1,0:T(8,128)(2,1)} async-done(((bf16[8,64,2048]{2,1,0:T(8,128)(2,1)}), bf16[32,64,2048]{2,1,0:T(8,128)(2,1)}) %all-gather.3.cloned.1.call-update) | async-done | bytes 8388624 | tf_op jit(solution)/shard_map/all_gather | solution.py:54
  162.2 5.6 %fusion.1 = f32[32,8,64]{2,1,0:T(8,128)S(1)} fusion(bf16[32,64,2048]{2,1,0:T(8,128)(2,1)} %all-gather.3.cloned.1.call-done, bf16[256,2048]{1,0:T(8,128)(2,1)S(1)} %scatter_custom_fusion), kind=kOutput, calls=%fused_computation.4 | convolution fusion | flops 67108864 | bytes 9502720 | tf_op jit(solution)/shard_map/fex,fyx->fey/dot_general | solution.py:10
  167.9 13.2 %psum.7 = bf16[32,8,64]{2,1,0:T(8,128)(2,1)S(1)} all-reduce(f32[32,8,64]{2,1,0:T(8,128)S(1)} %fusion.1), channel_id=1, replica_groups=mesh['group'=2,'dp'=4,'tensor'=4] {'tensor'}, use_global_device_ids=true, to_apply=%region_4.5 | all-reduce | flops 16384 | bytes 98304 | tf_op jit(solution)/shard_map/psum | solution.py:13
  181.0 130.7 %all-gather.5.cloned.1.call-done = bf16[32,64,2048]{2,1,0:T(8,128)(2,1)} async-done(((bf16[8,64,2048]{2,1,0:T(8,128)(2,1)}), bf16[32,64,2048]{2,1,0:T(8,128)(2,1)}) %all-gather.5.cloned.1.call-update) | async-done | bytes 8388624 | tf_op jit(solution)/shard_map/all_gather | solution.py:55
  311.8 4.6 %fusion = bf16[256,2048]{1,0:T(8,128)(2,1)S(1)} fusion(bf16[32,64,2048]{2,1,0:T(8,128)(2,1)} %all-gather.5.cloned.1.call-done, bf16[32,8,64]{2,1,0:T(8,128)(2,1)S(1)} %psum.7), kind=kOutput, calls=%fused_computation.3 | convolution fusion | flops 67633152 | bytes 9469952 | tf_op jit(solution)/shard_map/zxb,zbl->zxl/dot_general | solution.py:14
  316.3 0.9 gather_fusion
  317.3 0.3 copy.18
  317.6 0.0 reduce-scatter.2.cloned.1.call-done
  317.6 1.4 fusion.4
  319.0 1.0 copy.19
  (6 shorter events, 0.0 us)
Async XLA Ops:
  7.4 154.8 %all-gather.3.cloned.1.call-start = ((), (), s32[]{:S(2)}) async-start(), calls=%async_computation.2 | async-start | bytes 10485760 | tf_op jit(solution)/shard_map/all_gather | solution.py:54
  8.1 303.7 %all-gather.5.cloned.1.call-start = ((), (), s32[]{:S(2)}) async-start(), calls=%async_computation.3 | async-start | bytes 10485760 | tf_op jit(solution)/shard_map/all_gather | solution.py:55
  8.8 17.1 %copy-start = (bf16[128,2048]{1,0:T(8,128)(2,1)S(1)}, bf16[128,2048]{1,0:T(8,128)(2,1)}, u32[]{:S(2)}) copy-start(bf16[128,2048]{1,0:T(8,128)(2,1)} %param.8) | copy-start | bytes 1572868
  8.8 17.4 %copy-start.1 = (s32[128,1]{0,1:T(1,128)S(1)}, s32[128,1]{0,1:T(1,128)}, u32[]{:S(2)}) copy-start(s32[128,1]{0,1:T(1,128)} %param.12) | copy-start | bytes 1540
  8.9 17.4 %copy-start.2 = (s32[32]{0:T(128)S(1)}, s32[32]{0:T(128)}, u32[]{:S(2)}) copy-start(s32[32]{0:T(128)} %param.13) | copy-start | bytes 388
  8.9 308.7 %reduce-scatter.2.cloned.1.call-start = ((), (), s32[]{:S(2)}) async-start(), calls=%async_computation.1 | async-start | bytes 5242880 | tf_op jit(solution)/shard_map/reduce_scatter | solution.py:32
Sparse Core Ops, SparseCore 0:
  9.8 152.3 all-gather.2
  163.9 147.8 all-gather.4
Sparse Core Ops, SparseCore 1:
  26.0 48.1 reduce-scatter.1
where the time goes:
time: 328 us; the launch traced here: 327 us
  waiting for transfers between devices  266 us (81%)
  matrix products  27.2 us (8%)
  between operations  15 us (5%)
  blocking collectives  13.2 us (4%)
  local copies, waits for them, and re-layouts  4.73 us (1%)
    all_gather x1, waiting for transfers between devices, per_device(): lax.all_gather(low_rank_shrink, 'dp', axis=0, tiled=True)  133 us
    all_gather x1, waiting for transfers between devices, per_device(): lax.all_gather(low_rank_expand, 'dp', axis=0, tiled=True)  131 us
    dot_general x1, matrix products, per_device(): lax.dot_general(output_weight, attended, (((0,), (1,)), ((), ())), prefer...  17 us
    psum x1, blocking collectives, apply_low_rank(): shrunk_rows = lax.psum(partial_rank, 'tensor').astype(jnp.bfloat16)  13.2 us
  transfers between devices with their start and end apart: 3, of which 2 were waited for; matrix products, arithmetic and copies ran while one was open for 10% of the time, Pallas kernels for 0%

commit v1 on v0

v1 whole, which is shorter than its diff:
```python
import functools

import jax
import jax.numpy as jnp
from jax import lax
from jax.experimental import pallas as pl
from jax.experimental.pallas import tpu as pltpu
from jax.sharding import PartitionSpec as P

MESH = pl.DeviceIdType.MESH
ADAPTER_ROW_CAP = 8
CHUNKS = 2
RING = 4
F32 = jnp.float32
BF16 = jnp.bfloat16


def kernel(
    n_dp, n_t, cap,
    att, idx, slots, hid_hbm, w_hbm, shr_hbm, exp_hbm,
    out,
    sel, hold, recv, meta, metar, slc, zs, zr, dl, ret,
    wbuf, psend, precv, own, xsend, xrecv, hid, shr, exp,
    w_sem, in_sem, f_ss, f_rs, m_ss, m_rs, z_ss, z_rs, r_ss, r_rs, p_ss, p_rs, x_ss, x_rs,
):
    rows, width = att.shape
    store = shr.shape[0]
    n_x = n_t // 2
    n_j, tile = own.shape[1], own.shape[3]
    block = n_j * tile
    per_slot = store // (cap // ADAPTER_ROW_CAP)
    n_slots = store // per_slot
    ch = cap // CHUNKS
    wide = n_dp * ch
    d = lax.axis_index("dp")
    t = lax.axis_index("tensor")
    x, c = t // 2, lax.rem(t, 2)
    sibling = {"tensor": x * 2 + (1 - c)}

    def dp_at(off):
        return {"dp": lax.rem(d + off, n_dp)}

    def t_at(off):
        return {"tensor": lax.rem(t + off, n_t)}

    def w_copy(g, slot):
        i, h, j = g // (2 * n_j), lax.rem(g // n_j, 2), lax.rem(g, n_j)
        core = jnp.where(h == 0, 1 - c, c)
        dest = lax.rem(x + 1 + i, n_x) * 2 + core
        start = pl.multiple_of(dest * block + j * tile, tile)
        return pltpu.make_async_copy(w_hbm.at[:, pl.ds(start, tile)], wbuf.at[slot], w_sem.at[slot])

    barrier = pltpu.get_barrier_semaphore()
    for off in range(1, n_dp):
        pl.semaphore_signal(barrier, inc=1, device_id=dp_at(off), device_id_type=MESH)
    for off in range(1, n_t):
        pl.semaphore_signal(barrier, inc=1, device_id=t_at(off), device_id_type=MESH)

    for g in range(RING):
        w_copy(jnp.int32(g), g).start()
    loads = [
        pltpu.make_async_copy(shr_hbm, shr, in_sem.at[0]),
        pltpu.make_async_copy(exp_hbm, exp, in_sem.at[1]),
        pltpu.make_async_copy(hid_hbm, hid, in_sem.at[2]),
    ]
    for load in loads:
        load.start()

    n_ad = slots.shape[1]
    match = idx[...] == lax.broadcasted_iota(jnp.int32, (rows, n_ad), 1)
    slot = jnp.sum(jnp.where(match, slots[...].astype(F32), 0.0), axis=1, keepdims=True)
    owner = jnp.zeros((rows, 1), F32)
    for o in range(1, n_dp):
        owner = owner + jnp.where(slot >= float(o * n_slots), 1.0, 0.0)
    local = slot - owner * n_slots
    rel = owner - d.astype(F32)
    rel = jnp.where(rel < 0, rel + n_dp, rel)
    lane = lax.broadcasted_iota(jnp.int32, (rows, 128), 1).astype(F32)
    to_owner = lane == rel
    before = (
        lax.broadcasted_iota(jnp.int32, (rows, rows), 1)
        < lax.broadcasted_iota(jnp.int32, (rows, rows), 0)
    )
    earlier = jnp.dot(
        jnp.where(before, 1.0, 0.0).astype(BF16),
        jnp.where(to_owner, 1.0, 0.0).astype(BF16),
        preferred_element_type=F32,
    )
    place = jnp.sum(jnp.where(to_owner, earlier, 0.0), axis=1, keepdims=True)
    target = place + rel * ch
    for k in range(1, CHUNKS):
        target = target + jnp.where(place >= float(k * ch), float(wide - ch), 0.0)
    columns = lax.broadcasted_iota(jnp.int32, (rows, CHUNKS * wide), 1).astype(F32)
    sel[...] = jnp.where(columns == target, 1.0, 0.0).astype(BF16)
    for off in range(n_dp):
        here = jnp.where((lane == place) & (rel == float(off)), local, 0.0)
        row = jnp.broadcast_to(jnp.sum(here, axis=0, keepdims=True), (8, 128))
        if off == 0:
            metar[0] = row
        else:
            meta[off] = row

    fw = min(512, width)
    for k in range(CHUNKS):
        for f in range(width // fw):
            cols = pl.ds(f * fw, fw)
            part = lax.dot_general(
                sel[:, k * wide : (k + 1) * wide], att[:, cols], (((0,), (0,)), ((), ())),
                preferred_element_type=F32,
            ).astype(BF16)
            recv[k, pl.ds(0, ch), cols] = part[:ch]
            hold[k, pl.ds(ch, wide - ch), cols] = part[ch:]

    pl.semaphore_wait(barrier, n_dp + n_t - 2)

    order = sorted(range(1, n_dp), key=lambda off: -min(off, n_dp - off))

    def f_copy(k, off):
        return pltpu.make_async_remote_copy(
            src_ref=hold.at[k, pl.ds(off * ch, ch)], dst_ref=recv.at[k, pl.ds(off * ch, ch)],
            send_sem=f_ss.at[k, off], recv_sem=f_rs.at[k, off],
            device_id=dp_at(off), device_id_type=MESH,
        )

    def m_copy(off):
        return pltpu.make_async_remote_copy(
            src_ref=meta.at[off], dst_ref=metar.at[off],
            send_sem=m_ss.at[off], recv_sem=m_rs.at[off],
            device_id=dp_at(off), device_id_type=MESH,
        )

    def z_copy(k, off):
        return pltpu.make_async_remote_copy(
            src_ref=zs.at[k], dst_ref=zr.at[k, off],
            send_sem=z_ss.at[k, off], recv_sem=z_rs.at[k, off],
            device_id=t_at(off), device_id_type=MESH,
        )

    def r_copy(k, off):
        return pltpu.make_async_remote_copy(
            src_ref=dl.at[k, pl.ds(off * ch, ch)], dst_ref=ret.at[k, pl.ds(off * ch, ch)],
            send_sem=r_ss.at[k, off], recv_sem=r_rs.at[k, off],
            device_id=dp_at(n_dp - off), device_id_type=MESH,
        )

    def p_copy(i):
        return pltpu.make_async_remote_copy(
            src_ref=psend.at[i], dst_ref=precv.at[i],
            send_sem=p_ss.at[i], recv_sem=p_rs.at[i],
            device_id=sibling, device_id_type=MESH,
        )

    def x_copy(i):
        return pltpu.make_async_remote_copy(
            src_ref=xsend.at[i], dst_ref=xrecv.at[i],
            send_sem=x_ss.at[i], recv_sem=x_rs.at[i],
            device_id={"tensor": lax.rem(x + 1 + i, n_x) * 2 + c}, device_id_type=MESH,
        )

    for off in order:
        m_copy(off).start()
    for k in range(CHUNKS):
        for off in order:
            f_copy(k, off).start()

    tiles = n_t * n_j

    def product(g):
        at = lax.rem(g, RING)
        w_copy(g, at).wait()
        part = jnp.dot(att[...], wbuf[at], preferred_element_type=F32)

        return part, at

    def refill(g, at):
        @pl.when(g + RING < tiles)
        def _():
            w_copy(g + RING, at).start()

    def blocks(i):
        def first(j, carry):
            g = i * 2 * n_j + j
            part, at = product(g)
            psend[i, j] = part
            refill(g, at)
            return carry

        lax.fori_loop(0, n_j, first, 0)
        p_copy(i).start()

        def second(j, carry):
            g = i * 2 * n_j + n_j + j
            part, at = product(g)
            own[i, j] = part
            refill(g, at)
            return carry

        lax.fori_loop(0, n_j, second, 0)
        p_copy(i).wait_recv()

    def far(i, carry):
        blocks(i)

        def add(j, inner):
            xsend[i, j] = (own[i, j] + precv[i, j]).astype(BF16)
            return inner

        lax.fori_loop(0, n_j, add, 0)
        x_copy(i).start()
        return carry

    lax.fori_loop(0, n_x - 1, far, 0)
    blocks(jnp.int32(n_x - 1))

    for load in loads:
        load.wait()
    for off in order:
        m_copy(off).wait_recv()
    n_q = store // 128
    per = 128 // per_slot
    half = lax.broadcasted_iota(jnp.int32, (wide, 128), 1) // per_slot
    half = half.astype(F32)
    for k in range(CHUNKS):
        r_i = lax.broadcasted_iota(jnp.int32, (ch, 128), 0) + k * ch
        pick = lax.broadcasted_iota(jnp.int32, (ch, 128), 1) == r_i
        for off in range(n_dp):
            col = jnp.sum(jnp.where(pick, metar[off, 0:1, :], 0.0), axis=1, keepdims=True)
            slc[k, pl.ds(off * ch, ch)] = jnp.broadcast_to(col, (ch, 128))

    for k in range(CHUNKS):
        for off in order:
            f_copy(k, off).wait_recv()
        y = lax.dot_general(
            recv[k], shr[...], (((1,), (1,)), ((), ())), preferred_element_type=F32
        )
        z = jnp.zeros((wide, 128), F32)
        for q in range(n_q):
            z = z + jnp.where(slc[k] == half + float(q * per), y[:, q * 128 : (q + 1) * 128], 0.0)
        zs[k] = z
        for off in range(1, n_t):
            z_copy(k, off).start()
        for off in range(1, n_t):
            z_copy(k, off).wait_recv()
        total = zs[k]
        for off in range(1, n_t):
            total = total + zr[k, off]
        mixed = [
            jnp.where(slc[k] == half + float(q * per), total, 0.0).astype(BF16) for q in range(n_q)
        ]
        lhs = jnp.concatenate(mixed, axis=1)
        for f in range(width // fw):
            cols = pl.ds(f * fw, fw)
            part = jnp.dot(lhs, exp[:, cols], preferred_element_type=F32).astype(BF16)
            ret[k, pl.ds(0, ch), cols] = part[:ch]
            dl[k, pl.ds(ch, wide - ch), cols] = part[ch:]
        for off in order:
            r_copy(k, off).start()

    for i in range(n_x - 1):
        x_copy(i).wait_recv()
    for j in range(n_j):
        cols = pl.ds(j * tile, tile)
        total = own[n_x - 1, j] + precv[n_x - 1, j]
        for i in range(n_x - 1):
            total = total + xrecv[i, j].astype(F32)
        own[n_x - 1, j] = hid[:, cols].astype(F32) + total

    for k in range(CHUNKS):
        for off in order:
            r_copy(k, off).wait_recv()
    for j in range(n_j):
        cols = pl.ds(j * tile, tile)
        delta = own[n_x - 1, j]
        for k in range(CHUNKS):
            delta = delta + jnp.dot(
                sel[:, k * wide : (k + 1) * wide], ret[k, :, cols], preferred_element_type=F32
            )
        out[:, cols] = delta.astype(BF16)

    for off in order:
        m_copy(off).wait_send()
        for k in range(CHUNKS):
            f_copy(k, off).wait_send()
            r_copy(k, off).wait_send()
    for k in range(CHUNKS):
        for off in range(1, n_t):
            z_copy(k, off).wait_send()
    for i in range(n_x):
        p_copy(i).wait_send()
    for i in range(n_x - 1):
        x_copy(i).wait_send()


def solution(mesh):
    n_dp, n_t = mesh.shape["dp"], mesh.shape["tensor"]
    n_x = n_t // 2

    def per_device(attended, hidden, weight, shrink, expand, row_adapter, store_slot):
        rows, width = attended.shape
        n_slots, rank, _ = shrink.shape
        cap = n_slots * ADAPTER_ROW_CAP
        ch = cap // CHUNKS
        wide = n_dp * ch
        depth, total = weight.shape
        block = total // n_t
        tile = min(512, block)
        n_j = block // tile
        any_space = pl.BlockSpec(memory_space=pl.ANY)
        vmem = pl.BlockSpec(memory_space=pltpu.VMEM)
        dma = pltpu.SemaphoreType.DMA
        return pl.pallas_call(
            functools.partial(kernel, n_dp, n_t, cap),
            out_shape=jax.ShapeDtypeStruct((rows, width), BF16),
            in_specs=[vmem, vmem, vmem, any_space, any_space, any_space, any_space],
            out_specs=vmem,
            scratch_shapes=[
                pltpu.VMEM((rows, CHUNKS * wide), BF16),
                pltpu.VMEM((CHUNKS, wide, width), BF16),
                pltpu.VMEM((CHUNKS, wide, width), BF16),
                pltpu.VMEM((n_dp, 8, 128), F32),
                pltpu.VMEM((n_dp, 8, 128), F32),
                pltpu.VMEM((CHUNKS, wide, 128), F32),
                pltpu.VMEM((CHUNKS, wide, 128), F32),
                pltpu.VMEM((CHUNKS, n_t, wide, 128), F32),
                pltpu.VMEM((CHUNKS, wide, width), BF16),
                pltpu.VMEM((CHUNKS, wide, width), BF16),
                pltpu.VMEM((RING, depth, tile), BF16),
                pltpu.VMEM((n_x, n_j, rows, tile), F32),
                pltpu.VMEM((n_x, n_j, rows, tile), F32),
                pltpu.VMEM((n_x, n_j, rows, tile), F32),
                pltpu.VMEM((n_x - 1, n_j, rows, tile), BF16),
                pltpu.VMEM((n_x - 1, n_j, rows, tile), BF16),
                pltpu.VMEM((rows, width), BF16),
                pltpu.VMEM((n_slots * rank, width), BF16),
                pltpu.VMEM((n_slots * rank, width), BF16),
                dma((RING,)), dma((3,)),
                dma((CHUNKS, n_dp)), dma((CHUNKS, n_dp)), dma((n_dp,)), dma((n_dp,)),
                dma((CHUNKS, n_t)), dma((CHUNKS, n_t)), dma((CHUNKS, n_dp)), dma((CHUNKS, n_dp)),
                dma((n_x,)), dma((n_x,)), dma((n_x,)), dma((n_x,)),
            ],
            compiler_params=pltpu.CompilerParams(
                collective_id=0, has_side_effects=True, vmem_limit_bytes=48 * 1024 * 1024
            ),
        )(
            attended, row_adapter, store_slot.reshape(1, -1), hidden, weight,
            shrink.reshape(n_slots * rank, width), expand.reshape(n_slots * rank, width),
        )

    placed = (
        P(("group", "dp"), "tensor"),
        P(("group", "dp"), "tensor"),
        P("tensor", None),
        P(("group", "dp"), None, "tensor"),
        P(("group", "dp"), None, "tensor"),
        P(("group", "dp"), None),
        P("group"),
    )
    return jax.shard_map(
        per_device,
        mesh=mesh,
        in_specs=placed,
        out_specs=P(("group", "dp"), "tensor"),
        check_vma=False,
    )
```

time: 328 us -> 58.7 us (0.18)
  waiting for transfers between devices: 266 us -> 0 us
  Pallas kernels: 0 us -> 50.2 us
  matrix products: 27.2 us -> 0 us
  between operations: 15 us -> 0.02 us
  blocking collectives: 13.2 us -> 0 us
    all_gather x2 -> x0, waiting for transfers between devices: 264 us -> none  [the longest x1 133 us: per_device(): lax.all_gather(low_rank_shrink, 'dp', axis=0, tiled=True)]
    pallas_call x0 -> x1, Pallas kernels: none -> 50.2 us  [per_device(): pl.pallas_call(functools.partial(kernel, n_dp, n_t, cap), out_shape=jax.S...]
    dot_general x3 -> x0, matrix products: 27.2 us -> none  [the longest x1 17 us: per_device(): lax.dot_general(output_weight, attended, (((0,), (1,)), ((), ())), prefer...]
    psum x1 -> x0, blocking collectives: 13.2 us -> none  [apply_low_rank(): shrunk_rows = lax.psum(partial_rank, 'tensor').astype(jnp.bfloat16)]
    unnamed x7 -> x12, local copies, waits for them, and re-layouts: 0.29 us -> 7.47 us
  transfers between devices with their start and end apart: 3 -> 0, of which waited for: 2 -> 0; matrix products, arithmetic and copies ran while one was open for 10% -> 0% of each run, Pallas kernels for 0% -> 0%
where the time goes in v1:
time: 58.7 us; the launch traced here: 57.7 us
  Pallas kernels  50.2 us (86%)
  local copies, waits for them, and re-layouts  7.47 us (13%)
    pallas_call x1, Pallas kernels, per_device(): pl.pallas_call(functools.partial(kernel, n_dp, n_t, cap), out_shape=jax.S...  50.2 us
    unnamed x12, local copies, waits for them, and re-layouts  7.47 us

profile of v1, /device:TPU:0, one launch (start us, length us, event | category | flops | bytes accessed | tf_op | source)
XLA Modules:
  0.0 57.7 jit_solution(5898774726842583561)
XLA Ops:
  0.0 0.8 %copy.8.idx = s32[128,1]{1,0:T(8,128)S(1)} copy(s32[128,1]{0,1:T(1,128)} %param.12) | data formatting | bytes 1024 | tf_op args[5]
  0.8 0.0 copy-start
  0.8 1.6 %copy-done = bf16[8,64,2048]{2,1,0:T(8,128)(2,1)S(1)} copy-done((bf16[8,64,2048]{2,1,0:T(8,128)(2,1)S(1)}, bf16[8,64,2048]{2,1,0:T(8,128)(2,1)}, u32[]{:S(2)}) %copy-start) | copy-done | bytes 2097176
  2.4 0.0 copy-start.1
  2.4 1.6 %copy-done.1 = bf16[8,64,2048]{2,1,0:T(8,128)(2,1)S(1)} copy-done((bf16[8,64,2048]{2,1,0:T(8,128)(2,1)S(1)}, bf16[8,64,2048]{2,1,0:T(8,128)(2,1)}, u32[]{:S(2)}) %copy-start.1) | copy-done | bytes 2097176
  3.9 0.0 copy-start.2
  3.9 1.0 %copy-done.2 = bf16[128,2048]{1,0:T(8,128)(2,1)S(1)} copy-done((bf16[128,2048]{1,0:T(8,128)(2,1)S(1)}, bf16[128,2048]{1,0:T(8,128)(2,1)}, u32[]{:S(2)}) %copy-start.2) | copy-done | bytes 524312
  5.0 0.0 copy-start.3
  5.0 1.0 %copy-done.3 = bf16[128,2048]{1,0:T(8,128)(2,1)S(1)} copy-done((bf16[128,2048]{1,0:T(8,128)(2,1)S(1)}, bf16[128,2048]{1,0:T(8,128)(2,1)}, u32[]{:S(2)}) %copy-start.3) | copy-done | bytes 524312
  6.0 0.0 copy-start.4
  6.0 0.7 %copy-done.4 = s32[32]{0:T(128)S(1)} copy-done((s32[32]{0:T(128)S(1)}, s32[32]{0:T(128)}, u32[]{:S(2)}) %copy-start.4) | copy-done | bytes 152
  6.7 50.2 %shard_map.73 = bf16[128,2048]{1,0:T(8,128)(2,1)S(1)} custom-call(bf16[128,2048]{1,0:T(8,128)(2,1)S(1)} %copy-done.2, s32[128,1]{1,0:T(8,128)S(1)} %copy.8.idx, s32[1,32]{1,0:T(1,128)S(1)} %bitcast.5, bf16[128,2048]{1,0:T(8,128)(2,1)S(1)} %copy-done.3, bf16[2048,8192]{1,0:T(8,128)(2,1)} %w_hbm.1, bf16[512,2048]{1,0:T(8,128)(2,1)S(1)} %bitcast.3, ...), custom_call_target="tpu_custom_call" | custom-call | tf_op jit(solution)/shard_map/pallas_call | solution.py:311
  56.9 0.8 %copy.10 = bf16[128,2048]{1,0:T(8,128)(2,1)} copy(bf16[128,2048]{1,0:T(8,128)(2,1)S(1)} %shard_map.73) | data formatting | bytes 1048576
Async XLA Ops:
  0.8 1.6 %copy-start = (bf16[8,64,2048]{2,1,0:T(8,128)(2,1)S(1)}, bf16[8,64,2048]{2,1,0:T(8,128)(2,1)}, u32[]{:S(2)}) copy-start(bf16[8,64,2048]{2,1,0:T(8,128)(2,1)} %param.10) | copy-start | bytes 6291460
  2.4 1.6 %copy-start.1 = (bf16[8,64,2048]{2,1,0:T(8,128)(2,1)S(1)}, bf16[8,64,2048]{2,1,0:T(8,128)(2,1)}, u32[]{:S(2)}) copy-start(bf16[8,64,2048]{2,1,0:T(8,128)(2,1)} %param.11) | copy-start | bytes 6291460
  3.9 1.0 %copy-start.2 = (bf16[128,2048]{1,0:T(8,128)(2,1)S(1)}, bf16[128,2048]{1,0:T(8,128)(2,1)}, u32[]{:S(2)}) copy-start(bf16[128,2048]{1,0:T(8,128)(2,1)} %att.1) | copy-start | bytes 1572868
  5.0 1.0 %copy-start.3 = (bf16[128,2048]{1,0:T(8,128)(2,1)S(1)}, bf16[128,2048]{1,0:T(8,128)(2,1)}, u32[]{:S(2)}) copy-start(bf16[128,2048]{1,0:T(8,128)(2,1)} %hid_hbm.1) | copy-start | bytes 1572868
  6.0 0.7 %copy-start.4 = (s32[32]{0:T(128)S(1)}, s32[32]{0:T(128)}, u32[]{:S(2)}) copy-start(s32[32]{0:T(128)} %param.13) | copy-start | bytes 388

commit v2 on v1

v2 whole, which is shorter than its diff:
```python
import functools

import jax
import jax.numpy as jnp
from jax import lax
from jax.experimental import pallas as pl
from jax.experimental.pallas import tpu as pltpu
from jax.sharding import PartitionSpec as P

MESH = pl.DeviceIdType.MESH
ADAPTER_ROW_CAP = 8
RING = 4
F32 = jnp.float32
BF16 = jnp.bfloat16


def kernel(
    n_group, n_dp, n_t, n_slots, sizes, flagged,
    idx, slots, att_hbm, hid_hbm, w_hbm, shr_hbm, exp_hbm,
    out, over,
    att, flags, sel, hold, recv, meta, metar, slc, zs, zr, dl, ret,
    wbuf, psend, precv, own, xsend, xrecv, hid, shr, exp,
    w_sem, in_sem, f_ss, f_rs, m_ss, m_rs, z_ss, z_rs, r_ss, r_rs, p_ss, p_rs, x_ss, x_rs, o_ss, o_rs,
):
    rows, width = att.shape
    store = shr.shape[0]
    n_x = n_t // 2
    n_j, tile = own.shape[1], own.shape[3]
    block = n_j * tile
    per_slot = store // n_slots
    cap = sum(sizes)
    chunks = range(len(sizes))
    starts = [sum(sizes[:k]) for k in chunks]
    peers = n_group * n_dp if flagged else n_dp
    grp = lax.axis_index("group")
    d = lax.axis_index("dp")
    t = lax.axis_index("tensor")
    x, c = t // 2, lax.rem(t, 2)
    sibling = {"tensor": x * 2 + (1 - c)}

    def dp_at(off):
        return {"dp": lax.rem(d + off, n_dp)}

    def peer_at(off):
        if not flagged:
            return dp_at(off)
        to = lax.rem(grp * n_dp + d + off, peers)
        return {"group": to // n_dp, "dp": lax.rem(to, n_dp)}

    def part_of(k, off):
        return pl.ds(n_dp * starts[k] + off * sizes[k], sizes[k])

    def whole_of(k):
        return pl.ds(n_dp * starts[k], n_dp * sizes[k])

    def others_of(k):
        return pl.ds(n_dp * starts[k] + sizes[k], (n_dp - 1) * sizes[k])

    def t_at(off):
        return {"tensor": lax.rem(t + off, n_t)}

    def w_copy(g, slot):
        i, h, j = g // (2 * n_j), lax.rem(g // n_j, 2), lax.rem(g, n_j)
        core = jnp.where(h == 0, 1 - c, c)
        dest = lax.rem(x + 1 + i, n_x) * 2 + core
        start = pl.multiple_of(dest * block + j * tile, tile)
        return pltpu.make_async_copy(w_hbm.at[:, pl.ds(start, tile)], wbuf.at[slot], w_sem.at[slot])

    barrier = pltpu.get_barrier_semaphore()
    for off in range(1, peers):
        pl.semaphore_signal(barrier, inc=1, device_id=peer_at(off), device_id_type=MESH)
    for off in range(1, n_t):
        pl.semaphore_signal(barrier, inc=1, device_id=t_at(off), device_id_type=MESH)

    att_load = pltpu.make_async_copy(att_hbm, att, in_sem.at[3])
    att_load.start()
    for g in range(RING):
        w_copy(jnp.int32(g), g).start()
    loads = [
        pltpu.make_async_copy(shr_hbm, shr, in_sem.at[0]),
        pltpu.make_async_copy(exp_hbm, exp, in_sem.at[1]),
        pltpu.make_async_copy(hid_hbm, hid, in_sem.at[2]),
    ]
    for load in loads:
        load.start()

    n_ad = slots.shape[1]
    square = (rows, rows)
    across = lax.broadcasted_iota(jnp.int32, square, 1)
    down = lax.broadcasted_iota(jnp.int32, square, 0)
    named = jnp.sum(
        jnp.where(across == down, idx[...].astype(F32), 0.0), axis=1, keepdims=True
    ).astype(jnp.int32)
    match = named == lax.broadcasted_iota(jnp.int32, (rows, n_ad), 1)
    slot = jnp.sum(jnp.where(match, slots[...].astype(F32), 0.0), axis=1, keepdims=True)
    owner = jnp.zeros((rows, 1), F32)
    for o in range(1, n_dp):
        owner = owner + jnp.where(slot >= float(o * n_slots), 1.0, 0.0)
    local = slot - owner * n_slots
    rel = owner - d.astype(F32)
    rel = jnp.where(rel < 0, rel + n_dp, rel)
    lane = lax.broadcasted_iota(jnp.int32, (rows, 128), 1).astype(F32)
    to_owner = lane == rel
    before = across < down
    earlier = jnp.dot(
        jnp.where(before, 1.0, 0.0).astype(BF16),
        jnp.where(to_owner, 1.0, 0.0).astype(BF16),
        preferred_element_type=F32,
    )
    place = jnp.sum(jnp.where(to_owner, earlier, 0.0), axis=1, keepdims=True)
    target = place + rel * sizes[0]
    for k in chunks[1:]:
        later = place + rel * sizes[k] + float((n_dp - 1) * starts[k])
        target = jnp.where(place >= float(starts[k]), later, target)
    target = jnp.where(place >= float(cap), -1.0, target)
    columns = lax.broadcasted_iota(jnp.int32, (rows, n_dp * cap), 1).astype(F32)
    sel[...] = jnp.where(columns == target, 1.0, 0.0).astype(BF16)
    if flagged:
        most = jnp.max(jnp.where(place >= float(cap), 1.0, 0.0), axis=0, keepdims=True)
        flags[0] = jnp.broadcast_to(most, (8, 128))
    for off in range(n_dp):
        here = jnp.where((lane == place) & (rel == float(off)), local, 0.0)
        row = jnp.broadcast_to(jnp.sum(here, axis=0, keepdims=True), (8, 128))
        if off == 0:
            metar[0] = row
        else:
            meta[off] = row

    fw = min(512, width)
    order = sorted(range(1, n_dp), key=lambda off: -min(off, n_dp - off))

    def f_copy(k, off):
        return pltpu.make_async_remote_copy(
            src_ref=hold.at[part_of(k, off)], dst_ref=recv.at[part_of(k, off)],
            send_sem=f_ss.at[k, off], recv_sem=f_rs.at[k, off],
            device_id=dp_at(off), device_id_type=MESH,
        )

    def m_copy(off):
        return pltpu.make_async_remote_copy(
            src_ref=meta.at[off], dst_ref=metar.at[off],
            send_sem=m_ss.at[off], recv_sem=m_rs.at[off],
            device_id=dp_at(off), device_id_type=MESH,
        )

    def z_copy(k, off):
        return pltpu.make_async_remote_copy(
            src_ref=zs.at[whole_of(k)], dst_ref=zr.at[off, whole_of(k)],
            send_sem=z_ss.at[k, off], recv_sem=z_rs.at[k, off],
            device_id=t_at(off), device_id_type=MESH,
        )

    def r_copy(k, off):
        return pltpu.make_async_remote_copy(
            src_ref=dl.at[part_of(k, off)], dst_ref=ret.at[part_of(k, off)],
            send_sem=r_ss.at[k, off], recv_sem=r_rs.at[k, off],
            device_id=dp_at(n_dp - off), device_id_type=MESH,
        )

    def o_copy(off):
        return pltpu.make_async_remote_copy(
            src_ref=flags.at[0], dst_ref=flags.at[off],
            send_sem=o_ss.at[off], recv_sem=o_rs.at[off],
            device_id=peer_at(off), device_id_type=MESH,
        )

    def p_copy(i):
        return pltpu.make_async_remote_copy(
            src_ref=psend.at[i], dst_ref=precv.at[i],
            send_sem=p_ss.at[i], recv_sem=p_rs.at[i],
            device_id=sibling, device_id_type=MESH,
        )

    def x_copy(i):
        return pltpu.make_async_remote_copy(
            src_ref=xsend.at[i], dst_ref=xrecv.at[i],
            send_sem=x_ss.at[i], recv_sem=x_rs.at[i],
            device_id={"tensor": lax.rem(x + 1 + i, n_x) * 2 + c}, device_id_type=MESH,
        )

    att_load.wait()
    for k in chunks:
        own_rows, other_rows = sizes[k], others_of(k)
        for f in range(width // fw):
            cols = pl.ds(f * fw, fw)
            part = lax.dot_general(
                sel[:, whole_of(k)], att[:, cols], (((0,), (0,)), ((), ())),
                preferred_element_type=F32,
            ).astype(BF16)
            recv[part_of(k, 0), cols] = part[:own_rows]
            hold[other_rows, cols] = part[own_rows:]
        if k == 0:
            pl.semaphore_wait(barrier, peers + n_t - 2)
            for off in order:
                m_copy(off).start()
        for off in order:
            f_copy(k, off).start()
    if flagged:
        for off in range(1, peers):
            o_copy(off).start()

    tiles = n_t * n_j

    def product(g):
        at = lax.rem(g, RING)
        w_copy(g, at).wait()
        part = jnp.dot(att[...], wbuf[at], preferred_element_type=F32)

        return part, at

    def refill(g, at):
        @pl.when(g + RING < tiles)
        def _():
            w_copy(g + RING, at).start()

    def blocks(i):
        def first(j, carry):
            g = i * 2 * n_j + j
            part, at = product(g)
            psend[i, j] = part
            refill(g, at)
            return carry

        lax.fori_loop(0, n_j, first, 0)
        p_copy(i).start()

        def second(j, carry):
            g = i * 2 * n_j + n_j + j
            part, at = product(g)
            own[i, j] = part
            refill(g, at)
            return carry

        lax.fori_loop(0, n_j, second, 0)
        p_copy(i).wait_recv()

    def far(i, carry):
        blocks(i)

        def add(j, inner):
            xsend[i, j] = (own[i, j] + precv[i, j]).astype(BF16)
            return inner

        lax.fori_loop(0, n_j, add, 0)
        x_copy(i).start()
        return carry

    lax.fori_loop(0, n_x - 1, far, 0)
    blocks(jnp.int32(n_x - 1))

    for load in loads:
        load.wait()
    for off in order:
        m_copy(off).wait_recv()
    n_q = store // 128
    per = 128 // per_slot
    halves = (lax.broadcasted_iota(jnp.int32, (n_dp * cap, 128), 1) // per_slot).astype(F32)
    for k in chunks:
        ch = sizes[k]
        r_i = lax.broadcasted_iota(jnp.int32, (ch, 128), 0) + starts[k]
        pick = lax.broadcasted_iota(jnp.int32, (ch, 128), 1) == r_i
        for off in range(n_dp):
            col = jnp.sum(jnp.where(pick, metar[off, 0:1, :], 0.0), axis=1, keepdims=True)
            slc[part_of(k, off)] = jnp.broadcast_to(col, (ch, 128))

    for k in chunks:
        ch, wide, here = sizes[k], n_dp * sizes[k], whole_of(k)
        half = halves[:wide]
        slot_of = slc[here]
        for off in order:
            f_copy(k, off).wait_recv()
        y = lax.dot_general(
            recv[here], shr[...], (((1,), (1,)), ((), ())), preferred_element_type=F32
        )
        z = jnp.zeros((wide, 128), F32)
        for q in range(n_q):
            z = z + jnp.where(slot_of == half + float(q * per), y[:, q * 128 : (q + 1) * 128], 0.0)
        zs[here] = z
        for off in range(1, n_t):
            z_copy(k, off).start()
        for off in range(1, n_t):
            z_copy(k, off).wait_recv()
        total = zs[here]
        for off in range(1, n_t):
            total = total + zr[off, here]
        spread = [
            jnp.where(slot_of == half + float(q * per), total, 0.0).astype(BF16) for q in range(n_q)
        ]
        lhs = jnp.concatenate(spread, axis=1)
        for f in range(width // fw):
            cols = pl.ds(f * fw, fw)
            part = jnp.dot(lhs, exp[:, cols], preferred_element_type=F32).astype(BF16)
            ret[part_of(k, 0), cols] = part[:ch]
            dl[others_of(k), cols] = part[ch:]
        for off in order:
            r_copy(k, off).start()

    for i in range(n_x - 1):
        x_copy(i).wait_recv()
    for j in range(n_j):
        cols = pl.ds(j * tile, tile)
        total = own[n_x - 1, j] + precv[n_x - 1, j]
        for i in range(n_x - 1):
            total = total + xrecv[i, j].astype(F32)
        own[n_x - 1, j] = hid[:, cols].astype(F32) + total

    if flagged:
        most = flags[0]
        for off in range(1, peers):
            o_copy(off).wait_recv()
            most = jnp.maximum(most, flags[off])
        over[...] = most
    else:
        over[...] = jnp.zeros((8, 128), F32)
    for k in chunks:
        for off in order:
            r_copy(k, off).wait_recv()
    for j in range(n_j):
        cols = pl.ds(j * tile, tile)
        delta = jnp.dot(sel[...], ret[:, cols], preferred_element_type=F32)
        out[:, cols] = (own[n_x - 1, j] + delta).astype(BF16)

    for off in order:
        m_copy(off).wait_send()
        for k in chunks:
            f_copy(k, off).wait_send()
            r_copy(k, off).wait_send()
    for k in chunks:
        for off in range(1, n_t):
            z_copy(k, off).wait_send()
    if flagged:
        for off in range(1, peers):
            o_copy(off).wait_send()
    for i in range(n_x):
        p_copy(i).wait_send()
    for i in range(n_x - 1):
        x_copy(i).wait_send()


def solution(mesh):
    n_group, n_dp, n_t = mesh.shape["group"], mesh.shape["dp"], mesh.shape["tensor"]
    n_x = n_t // 2

    def run(sizes, flagged, attended, hidden, weight, shrink, expand, row_adapter, store_slot):
        rows, width = attended.shape
        n_slots, rank, _ = shrink.shape
        cap = sum(sizes)
        lanes = n_dp * cap
        peers = n_group * n_dp
        depth, total = weight.shape
        block = total // n_t
        tile = min(512, block)
        n_j = block // tile
        any_space = pl.BlockSpec(memory_space=pl.ANY)
        vmem = pl.BlockSpec(memory_space=pltpu.VMEM)
        dma = pltpu.SemaphoreType.DMA
        return pl.pallas_call(
            functools.partial(kernel, n_group, n_dp, n_t, n_slots, sizes, flagged),
            out_shape=(
                jax.ShapeDtypeStruct((rows, width), BF16), jax.ShapeDtypeStruct((8, 128), F32)
            ),
            in_specs=[vmem, vmem] + [any_space] * 5,
            out_specs=(vmem, vmem),
            scratch_shapes=[
                pltpu.VMEM((rows, width), BF16),
                pltpu.VMEM((peers, 8, 128), F32),
                pltpu.VMEM((rows, lanes), BF16),
                pltpu.VMEM((lanes, width), BF16),
                pltpu.VMEM((lanes, width), BF16),
                pltpu.VMEM((n_dp, 8, 128), F32),
                pltpu.VMEM((n_dp, 8, 128), F32),
                pltpu.VMEM((lanes, 128), F32),
                pltpu.VMEM((lanes, 128), F32),
                pltpu.VMEM((n_t, lanes, 128), F32),
                pltpu.VMEM((lanes, width), BF16),
                pltpu.VMEM((lanes, width), BF16),
                pltpu.VMEM((RING, depth, tile), BF16),
                pltpu.VMEM((n_x, n_j, rows, tile), F32),
                pltpu.VMEM((n_x, n_j, rows, tile), F32),
                pltpu.VMEM((n_x, n_j, rows, tile), F32),
                pltpu.VMEM((n_x - 1, n_j, rows, tile), BF16),
                pltpu.VMEM((n_x - 1, n_j, rows, tile), BF16),
                pltpu.VMEM((rows, width), BF16),
                pltpu.VMEM((n_slots * rank, width), BF16),
                pltpu.VMEM((n_slots * rank, width), BF16),
                dma((RING,)), dma((4,)),
                dma((len(sizes), n_dp)), dma((len(sizes), n_dp)), dma((n_dp,)), dma((n_dp,)),
                dma((len(sizes), n_t)), dma((len(sizes), n_t)), dma((len(sizes), n_dp)), dma((len(sizes), n_dp)),
                dma((n_x,)), dma((n_x,)), dma((n_x,)), dma((n_x,)),
                dma((peers,)), dma((peers,)),
            ],
            compiler_params=pltpu.CompilerParams(
                collective_id=0 if flagged else 1,
                has_side_effects=True,
                vmem_limit_bytes=60 * 1024 * 1024,
            ),
        )(
            row_adapter.reshape(1, -1), store_slot.reshape(1, -1), attended, hidden, weight,
            shrink.reshape(n_slots * rank, width), expand.reshape(n_slots * rank, width),
        )

    def per_device(*blocks):
        bound = blocks[3].shape[0] * ADAPTER_ROW_CAP
        most = (bound // 2, bound // 4)
        mixed, over = run(most, True, *blocks)
        return lax.cond(
            over[0, 0] > 0.5,
            lambda: run((bound // 2, bound // 2), False, *blocks)[0],
            lambda: mixed,
        )

    placed = (
        P(("group", "dp"), "tensor"),
        P(("group", "dp"), "tensor"),
        P("tensor", None),
        P(("group", "dp"), None, "tensor"),
        P(("group", "dp"), None, "tensor"),
        P(("group", "dp"), None),
        P("group"),
    )
    return jax.shard_map(
        per_device,
        mesh=mesh,
        in_specs=placed,
        out_specs=P(("group", "dp"), "tensor"),
        check_vma=False,
    )
```

time: 58.7 us -> 51.8 us (0.88); the launches traced: 57.7 us -> 51.6 us
  local copies, waits for them, and re-layouts: 7.47 us -> 2.01 us
  Pallas kernels: 50.2 us -> 48.8 us
  between operations: 0.02 us -> 0.72 us
    unnamed x12 -> x11, local copies, waits for them, and re-layouts: 7.47 us -> 0.81 us
    pallas_call x1, Pallas kernels: 50.2 us -> 48.8 us  [run(): pl.pallas_call(functools.partial(kernel, n_group, n_dp, n_t, n_slots, siz...]
    slice x0 -> x1, local copies, waits for them, and re-layouts: none -> 1.2 us  [per_device(): over[0, 0] > 0.5]
where the time goes in v2:
time: 51.8 us; the launch traced here: 51.6 us
  Pallas kernels  48.8 us (94%)
  local copies, waits for them, and re-layouts  2.01 us (4%)
  between operations  0.72 us (1%)
    pallas_call x1, Pallas kernels, run(): pl.pallas_call(functools.partial(kernel, n_group, n_dp, n_t, n_slots, siz...  48.8 us
    slice x1, local copies, waits for them, and re-layouts, per_device(): over[0, 0] > 0.5  1.2 us

profile of v2, /device:TPU:0, one launch (start us, length us, event | category | flops | bytes accessed | tf_op | source)
XLA Modules:
  0.0 51.6 jit_solution(9541796482500719087)
XLA Ops:
  0.0 0.0 copy-start
  0.0 0.0 copy-start.1
  0.0 0.0 copy-start.2
  0.0 0.0 copy-start.3
  0.0 0.0 copy-start.4
  0.0 48.8 %shard_map.75 = (bf16[128,2048]{1,0:T(8,128)(2,1)S(1)}, f32[8,128]{1,0:T(8,128)}) custom-call(s32[1,128]{1,0:T(1,128)} %bitcast.13, s32[1,32]{1,0:T(1,128)} %bitcast.15, bf16[128,2048]{1,0:T(8,128)(2,1)} %att_hbm.1, bf16[128,2048]{1,0:T(8,128)(2,1)} %hid_hbm.1, bf16[2048,8192]{1,0:T(8,128)(2,1)} %w_hbm.1, bf16[512,2048]{1,0:T(8,128)(2,1)} %bitcast.9, ...), custom_call_target="tpu_custom_call" | custom-call | tf_op jit(solution)/shard_map/pallas_call | solution.py:357
  48.9 1.2 %slice.3 = f32[1,1]{1,0:T(1,128)} slice(f32[8,128]{1,0:T(8,128)} %get-tuple-element.33), slice={[0:1], [0:1]} | slice | bytes 8 | tf_op jit(solution)/shard_map/slice | solution.py:407
  50.7 0.0 copy-done
  50.7 0.0 copy-done.1
  50.7 0.0 copy-done.2
  50.7 0.0 copy-done.3
  50.7 0.0 copy-done.4
  50.8 0.8 %copy.13 = bf16[128,2048]{1,0:T(8,128)(2,1)} copy(bf16[128,2048]{1,0:T(8,128)(2,1)S(1)} %get-tuple-element.35) | data formatting | bytes 1048576
  (1 shorter events, 0.0 us)
Async XLA Ops:
  0.0 50.7 %copy-start = (bf16[8,64,2048]{2,1,0:T(8,128)(2,1)S(1)}, bf16[8,64,2048]{2,1,0:T(8,128)(2,1)}, u32[]{:S(2)}) copy-start(bf16[8,64,2048]{2,1,0:T(8,128)(2,1)} %param.12) | copy-start | bytes 6291460
  0.0 50.7 %copy-start.1 = (bf16[128,2048]{1,0:T(8,128)(2,1)S(1)}, bf16[128,2048]{1,0:T(8,128)(2,1)}, u32[]{:S(2)}) copy-start(bf16[128,2048]{1,0:T(8,128)(2,1)} %att_hbm.1) | copy-start | bytes 1572868
  0.0 50.7 %copy-start.2 = (bf16[128,2048]{1,0:T(8,128)(2,1)S(1)}, bf16[128,2048]{1,0:T(8,128)(2,1)}, u32[]{:S(2)}) copy-start(bf16[128,2048]{1,0:T(8,128)(2,1)} %hid_hbm.1) | copy-start | bytes 1572868
  0.0 50.7 %copy-start.3 = (s32[128,1]{0,1:T(1,128)S(1)}, s32[128,1]{0,1:T(1,128)}, u32[]{:S(2)}) copy-start(s32[128,1]{0,1:T(1,128)} %param.14) | copy-start | bytes 1540
  0.0 50.7 %copy-start.4 = (s32[32]{0:T(128)S(1)}, s32[32]{0:T(128)}, u32[]{:S(2)}) copy-start(s32[32]{0:T(128)} %param.15) | copy-start | bytes 388

commit v3 on v2

--- a/solution.py
+++ b/solution.py
@@ -213,40 +213,45 @@
         def _():
             w_copy(g + RING, at).start()
 
-    def blocks(i):
-        def first(j, carry):
+    def first(i):
+        def step(j, carry):
             g = i * 2 * n_j + j
             part, at = product(g)
             psend[i, j] = part
             refill(g, at)
             return carry
 
-        lax.fori_loop(0, n_j, first, 0)
+        lax.fori_loop(0, n_j, step, 0)
         p_copy(i).start()
 
-        def second(j, carry):
+    def second(i):
+        def step(j, carry):
             g = i * 2 * n_j + n_j + j
             part, at = product(g)
             own[i, j] = part
             refill(g, at)
             return carry
 
-        lax.fori_loop(0, n_j, second, 0)
+        lax.fori_loop(0, n_j, step, 0)
         p_copy(i).wait_recv()
 
     def far(i, carry):
-        blocks(i)
+        first(i)
+        second(i)
 
         def add(j, inner):
             xsend[i, j] = (own[i, j] + precv[i, j]).astype(BF16)
             return inner
 
         lax.fori_loop(0, n_j, add, 0)
-        x_copy(i).start()
         return carry
 
+    def send_far():
+        for i in range(n_x - 1):
+            x_copy(i).start()
+
+    near = jnp.int32(n_x - 1)
     lax.fori_loop(0, n_x - 1, far, 0)
-    blocks(jnp.int32(n_x - 1))
 
     for load in loads:
         load.wait()
@@ -263,8 +268,8 @@
             col = jnp.sum(jnp.where(pick, metar[off, 0:1, :], 0.0), axis=1, keepdims=True)
             slc[part_of(k, off)] = jnp.broadcast_to(col, (ch, 128))
 
-    for k in chunks:
-        ch, wide, here = sizes[k], n_dp * sizes[k], whole_of(k)
+    def shrink(k):
+        wide, here = n_dp * sizes[k], whole_of(k)
         half = halves[:wide]
         slot_of = slc[here]
         for off in order:
@@ -278,6 +283,11 @@
         zs[here] = z
         for off in range(1, n_t):
             z_copy(k, off).start()
+
+    def expand(k):
+        ch, wide, here = sizes[k], n_dp * sizes[k], whole_of(k)
+        half = halves[:wide]
+        slot_of = slc[here]
         for off in range(1, n_t):
             z_copy(k, off).wait_recv()
         total = zs[here]
@@ -295,6 +305,17 @@
         for off in order:
             r_copy(k, off).start()
 
+    shrink(0)
+    first(near)
+    expand(0)
+    for k in chunks[1:]:
+        shrink(k)
+        if k == 1:
+            second(near)
+        if k == chunks[-1]:
+            send_far()
+        expand(k)
+
     for i in range(n_x - 1):
         x_copy(i).wait_recv()
     for j in range(n_j):
@@ -315,10 +336,16 @@
     for k in chunks:
         for off in order:
             r_copy(k, off).wait_recv()
-    for j in range(n_j):
-        cols = pl.ds(j * tile, tile)
-        delta = jnp.dot(sel[...], ret[:, cols], preferred_element_type=F32)
-        out[:, cols] = (own[n_x - 1, j] + delta).astype(BF16)
+        for j in range(n_j):
+            cols = pl.ds(j * tile, tile)
+            delta = jnp.dot(
+                sel[:, whole_of(k)], ret[whole_of(k), cols], preferred_element_type=F32
+            )
+            total = own[n_x - 1, j] + delta
+            if k == chunks[-1]:
+                out[:, cols] = total.astype(BF16)
+            else:
+                own[n_x - 1, j] = total
 
     for off in order:
         m_copy(off).wait_send()
@@ -401,7 +428,7 @@
 
     def per_device(*blocks):
         bound = blocks[3].shape[0] * ADAPTER_ROW_CAP
-        most = (bound // 2, bound // 4)
+        most = (bound // 4, bound // 2)
         mixed, over = run(most, True, *blocks)
         return lax.cond(
             over[0, 0] > 0.5,

time: 51.8 us -> 48.7 us (0.940)
  Pallas kernels: 48.8 us -> 45.4 us
    pallas_call x1, Pallas kernels: 48.8 us -> 45.4 us  [run(): pl.pallas_call(functools.partial(kernel, n_group, n_dp, n_t, n_slots, siz...]
where the time goes in v3:
time: 48.7 us; the launch traced here: 48.2 us
  Pallas kernels  45.4 us (93%)
  local copies, waits for them, and re-layouts  2.01 us (4%)
  between operations  0.72 us (1%)
    pallas_call x1, Pallas kernels, run(): pl.pallas_call(functools.partial(kernel, n_group, n_dp, n_t, n_slots, siz...  45.4 us
    slice x1, local copies, waits for them, and re-layouts, per_device(): over[0, 0] > 0.5  1.2 us

profile of v3, /device:TPU:0, one launch (start us, length us, event | category | flops | bytes accessed | tf_op | source)
XLA Modules:
  0.0 48.2 jit_solution(15757155692644266524)
XLA Ops:
  0.0 0.0 copy-start
  0.0 0.0 copy-start.1
  0.0 0.0 copy-start.2
  0.0 0.0 copy-start.3
  0.0 0.0 copy-start.4
  0.0 45.4 %shard_map.75 = (bf16[128,2048]{1,0:T(8,128)(2,1)S(1)}, f32[8,128]{1,0:T(8,128)}) custom-call(s32[1,128]{1,0:T(1,128)} %bitcast.13, s32[1,32]{1,0:T(1,128)} %bitcast.15, bf16[128,2048]{1,0:T(8,128)(2,1)} %att_hbm.1, bf16[128,2048]{1,0:T(8,128)(2,1)} %hid_hbm.1, bf16[2048,8192]{1,0:T(8,128)(2,1)} %w_hbm.1, bf16[512,2048]{1,0:T(8,128)(2,1)} %bitcast.9, ...), custom_call_target="tpu_custom_call" | custom-call | tf_op jit(solution)/shard_map/pallas_call | solution.py:384
  45.5 1.2 %slice.3 = f32[1,1]{1,0:T(1,128)} slice(f32[8,128]{1,0:T(8,128)} %get-tuple-element.33), slice={[0:1], [0:1]} | slice | bytes 8 | tf_op jit(solution)/shard_map/slice | solution.py:434
  47.3 0.0 copy-done
  47.3 0.0 copy-done.1
  47.3 0.0 copy-done.2
  47.3 0.0 copy-done.3
  47.3 0.0 copy-done.4
  47.4 0.8 %copy.13 = bf16[128,2048]{1,0:T(8,128)(2,1)} copy(bf16[128,2048]{1,0:T(8,128)(2,1)S(1)} %get-tuple-element.35) | data formatting | bytes 1048576
  (1 shorter events, 0.0 us)
Async XLA Ops:
  0.0 47.3 %copy-start = (bf16[8,64,2048]{2,1,0:T(8,128)(2,1)S(1)}, bf16[8,64,2048]{2,1,0:T(8,128)(2,1)}, u32[]{:S(2)}) copy-start(bf16[8,64,2048]{2,1,0:T(8,128)(2,1)} %param.12) | copy-start | bytes 6291460
  0.0 47.3 %copy-start.1 = (bf16[128,2048]{1,0:T(8,128)(2,1)S(1)}, bf16[128,2048]{1,0:T(8,128)(2,1)}, u32[]{:S(2)}) copy-start(bf16[128,2048]{1,0:T(8,128)(2,1)} %att_hbm.1) | copy-start | bytes 1572868
  0.0 47.3 %copy-start.2 = (bf16[128,2048]{1,0:T(8,128)(2,1)S(1)}, bf16[128,2048]{1,0:T(8,128)(2,1)}, u32[]{:S(2)}) copy-start(bf16[128,2048]{1,0:T(8,128)(2,1)} %hid_hbm.1) | copy-start | bytes 1572868
  0.0 47.3 %copy-start.3 = (s32[128,1]{0,1:T(1,128)S(1)}, s32[128,1]{0,1:T(1,128)}, u32[]{:S(2)}) copy-start(s32[128,1]{0,1:T(1,128)} %param.14) | copy-start | bytes 1540
  0.0 47.3 %copy-start.4 = (s32[32]{0:T(128)S(1)}, s32[32]{0:T(128)}, u32[]{:S(2)}) copy-start(s32[32]{0:T(128)} %param.15) | copy-start | bytes 388

commit v4 on v3

--- a/solution.py
+++ b/solution.py
@@ -330,9 +330,9 @@
         for off in range(1, peers):
             o_copy(off).wait_recv()
             most = jnp.maximum(most, flags[off])
-        over[...] = most
+        over[0, 0] = jnp.max(most)
     else:
-        over[...] = jnp.zeros((8, 128), F32)
+        over[0, 0] = jnp.float32(0.0)
     for k in chunks:
         for off in order:
             r_copy(k, off).wait_recv()
@@ -384,10 +384,10 @@
         return pl.pallas_call(
             functools.partial(kernel, n_group, n_dp, n_t, n_slots, sizes, flagged),
             out_shape=(
-                jax.ShapeDtypeStruct((rows, width), BF16), jax.ShapeDtypeStruct((8, 128), F32)
+                jax.ShapeDtypeStruct((rows, width), BF16), jax.ShapeDtypeStruct((1, 1), F32)
             ),
             in_specs=[vmem, vmem] + [any_space] * 5,
-            out_specs=(vmem, vmem),
+            out_specs=(vmem, pl.BlockSpec(memory_space=pltpu.SMEM)),
             scratch_shapes=[
                 pltpu.VMEM((rows, width), BF16),
                 pltpu.VMEM((peers, 8, 128), F32),

time: 48.7 us -> 47.4 us (0.973)
  local copies, waits for them, and re-layouts: 2.01 us -> 0.81 us
    slice x1 -> x0, local copies, waits for them, and re-layouts: 1.2 us -> none  [per_device(): over[0, 0] > 0.5]
where the time goes in v4:
time: 47.4 us; the launch traced here: 46.9 us
  Pallas kernels  45.4 us (96%)
  local copies, waits for them, and re-layouts  0.81 us (2%)
  between operations  0.74 us (2%)
    pallas_call x1, Pallas kernels, run(): pl.pallas_call(functools.partial(kernel, n_group, n_dp, n_t, n_slots, siz...  45.4 us

profile of v4, /device:TPU:0, one launch (start us, length us, event | category | flops | bytes accessed | tf_op | source)
XLA Modules:
  0.0 46.9 jit_solution(4983717244720893981)
XLA Ops:
  0.0 0.0 copy-start
  0.0 0.0 copy-start.1
  0.0 0.0 copy-start.2
  0.0 0.0 copy-start.3
  0.0 0.0 copy-start.4
  0.0 45.4 %shard_map.75 = (bf16[128,2048]{1,0:T(8,128)(2,1)S(1)}, f32[1,1]{1,0:T(1,128)}) custom-call(s32[1,128]{1,0:T(1,128)} %bitcast.13, s32[1,32]{1,0:T(1,128)} %bitcast.15, bf16[128,2048]{1,0:T(8,128)(2,1)} %att_hbm.1, bf16[128,2048]{1,0:T(8,128)(2,1)} %hid_hbm.1, bf16[2048,8192]{1,0:T(8,128)(2,1)} %w_hbm.1, bf16[512,2048]{1,0:T(8,128)(2,1)} %bitcast.9, ...), custom_call_target="tpu_custom_call" | custom-call | tf_op jit(solution)/shard_map/pallas_call | solution.py:384
  46.1 0.0 copy-done
  46.1 0.0 copy-done.1
  46.1 0.0 copy-done.2
  46.1 0.0 copy-done.3
  46.1 0.0 copy-done.4
  46.1 0.8 %copy.13 = bf16[128,2048]{1,0:T(8,128)(2,1)} copy(bf16[128,2048]{1,0:T(8,128)(2,1)S(1)} %get-tuple-element.35) | data formatting | bytes 1048576
  (1 shorter events, 0.0 us)
Async XLA Ops:
  0.0 46.1 %copy-start = (bf16[8,64,2048]{2,1,0:T(8,128)(2,1)S(1)}, bf16[8,64,2048]{2,1,0:T(8,128)(2,1)}, u32[]{:S(2)}) copy-start(bf16[8,64,2048]{2,1,0:T(8,128)(2,1)} %param.12) | copy-start | bytes 6291460
  0.0 46.1 %copy-start.1 = (bf16[128,2048]{1,0:T(8,128)(2,1)S(1)}, bf16[128,2048]{1,0:T(8,128)(2,1)}, u32[]{:S(2)}) copy-start(bf16[128,2048]{1,0:T(8,128)(2,1)} %att_hbm.1) | copy-start | bytes 1572868
  0.0 46.1 %copy-start.2 = (bf16[128,2048]{1,0:T(8,128)(2,1)S(1)}, bf16[128,2048]{1,0:T(8,128)(2,1)}, u32[]{:S(2)}) copy-start(bf16[128,2048]{1,0:T(8,128)(2,1)} %hid_hbm.1) | copy-start | bytes 1572868
  0.0 46.1 %copy-start.3 = (s32[128,1]{0,1:T(1,128)S(1)}, s32[128,1]{0,1:T(1,128)}, u32[]{:S(2)}) copy-start(s32[128,1]{0,1:T(1,128)} %param.14) | copy-start | bytes 1540
  0.0 46.1 %copy-start.4 = (s32[32]{0:T(128)S(1)}, s32[32]{0:T(128)}, u32[]{:S(2)}) copy-start(s32[32]{0:T(128)} %param.15) | copy-start | bytes 388
